TPU v7x, 32 devices: a whole 2x2x4 slice. The times are simulated.
32 devices in a mesh: wide: 8 (over z, x), narrow: 4 (over y, core).
Axes of the slice: x: 2, y: 2, z: 4, core: 2. Of those that a mesh axis runs over, the one named last changes fastest.
Arguments:
- state: float32 [12, 128, 64, 128], P(None, 'wide', 'narrow'), may hold values from -6 to 6
- wind_x: bfloat16 [128, 64, 128], P('wide', 'narrow'), may hold values from -8 to 8
- wind_y: bfloat16 [128, 64, 128], P('wide', 'narrow'), may hold values from -8 to 8
- level_mix: bfloat16 [128, 128], replicated, may hold values from -0.5 to 0.5
- field_mix: float32 [12, 12], replicated, may hold values from -1.75 to 1.75
- block_cost: int32 [16, 4], P('wide', 'narrow'), may hold values from 6 to 24
Outputs:
- new_state: float32 [12, 128, 64, 128], P(None, 'wide', 'narrow')
- tendency: float32 [12, 128, 64, 128], P(None, 'wide', 'narrow')
All inputs are finite; a program needn't handle non-finite values.
Results may differ from a plain program's by a relative error of at most 0.0012.
Values sent between devices are 32-bit elements; how exact they have to be, the bound alone decides.
A program may use at most 64 MiB of HBM per device.

v0:
```python
import functools
import math

import numpy as np
import jax
import jax.numpy as jnp
from jax import lax
from jax.experimental import pallas as pl
from jax.experimental.pallas import tpu as pltpu
from jax.sharding import PartitionSpec as P

NP = 4
NSUB = 4
BR = 8
MESH = pl.DeviceIdType.MESH

dyn_step = 0.05


def derivative_table():
    inner = 1.0 / math.sqrt(5.0)
    nodes = np.array([-1.0, -inner, inner, 1.0])
    identity = np.eye(4)
    spacing = nodes[:, None] - nodes[None, :] + identity
    barycentric = 1.0 / np.prod(spacing, axis=1)
    off_diag = barycentric[None, :] / barycentric[:, None] / spacing * (1.0 - identity)
    table = off_diag - identity * np.sum(off_diag, axis=1)[:, None]
    table[np.abs(table) < 1e-12] = 0.0
    return table


def micro_kernel(cost_ref, state_ref, level_ref, field_ref, raw_ref, sum_ref, work, mix_hi, mix_lo, levels2):
    fields, rows, columns, levels = state_ref.shape
    count_blocks = rows // BR
    half = BR // 2
    size = fields * columns

    levels2[...] = jnp.zeros_like(levels2)
    levels2[:levels, :levels] = level_ref[...]
    levels2[levels:, levels:] = level_ref[...]

    mix = field_ref[...]
    high = mix.astype(jnp.bfloat16)
    low = (mix - high.astype(jnp.float32)).astype(jnp.bfloat16)
    wide_row = lax.broadcasted_iota(jnp.int32, (size, fields), 0) // columns
    spread = (wide_row == lax.broadcasted_iota(jnp.int32, (size, fields), 1)).astype(jnp.float32).astype(jnp.bfloat16)
    wide_col = lax.broadcasted_iota(jnp.int32, (fields, size), 1) // columns
    spread_t = (wide_col == lax.broadcasted_iota(jnp.int32, (fields, size), 0)).astype(jnp.float32).astype(jnp.bfloat16)
    same = (
        lax.broadcasted_iota(jnp.int32, (size, size), 0) % columns
        == lax.broadcasted_iota(jnp.int32, (size, size), 1) % columns
    )
    for part, held in ((high, mix_hi), (low, mix_lo)):
        tall = jnp.dot(spread, part, preferred_element_type=jnp.float32).astype(jnp.bfloat16)
        full = jnp.dot(tall, spread_t, preferred_element_type=jnp.float32)
        held[...] = jnp.where(same, full, 0.0).astype(jnp.bfloat16)

    for block in range(count_blocks):
        for group in range(half):
            for side in range(2):
                row = block * BR + side * half + group
                work[block, group, :, side * levels:(side + 1) * levels] = (
                    state_ref[:, row].reshape(size, levels)
                )

    def turn(block, group):
        current = work[block, group]
        rounded = current.astype(jnp.bfloat16)
        coupled = jnp.dot(mix_hi[...], rounded, preferred_element_type=jnp.float32)
        coupled = coupled + jnp.dot(mix_lo[...], rounded, preferred_element_type=jnp.float32)
        top = coupled.astype(jnp.bfloat16)
        rest = (coupled - top.astype(jnp.float32)).astype(jnp.bfloat16)
        mixed = jnp.dot(top, levels2[...], preferred_element_type=jnp.float32)
        mixed = mixed + jnp.dot(rest, levels2[...], preferred_element_type=jnp.float32)
        work[block, group] = 0.5 * (current + jnp.tanh(mixed))

    counts = [cost_ref[block, 0] for block in range(count_blocks)]
    shared = functools.reduce(jnp.minimum, counts)

    def all_blocks(_, carry):
        for block in range(count_blocks):
            for group in range(half):
                turn(block, group)
        return carry

    lax.fori_loop(0, shared, all_blocks, 0)

    for block in range(count_blocks):
        def one_block(_, carry, block=block):
            for group in range(half):
                turn(block, group)
            return carry

        lax.fori_loop(shared, counts[block], one_block, 0)

    total = jnp.zeros((fields, levels), jnp.float32)
    for block in range(count_blocks):
        for group in range(half):
            for side in range(2):
                row = block * BR + side * half + group
                ended = work[block, group, :, side * levels:(side + 1) * levels]
                raw = ended.reshape(fields, columns, levels) - state_ref[:, row]
                raw_ref[:, row] = raw
                total = total + jnp.sum(raw, axis=1)
    sum_ref[...] = total


def microphysics(state, level_mix, field_mix, block_cost):
    fields, rows, columns, levels = state.shape
    size = fields * columns
    vmem = pl.BlockSpec(memory_space=pltpu.VMEM)
    return pl.pallas_call(
        micro_kernel,
        out_shape=(
            jax.ShapeDtypeStruct(state.shape, jnp.float32),
            jax.ShapeDtypeStruct((fields, levels), jnp.float32),
        ),
        in_specs=[pl.BlockSpec(memory_space=pltpu.SMEM), vmem, vmem, vmem],
        out_specs=(vmem, vmem),
        scratch_shapes=[
            pltpu.VMEM((rows // BR, BR // 2, size, 2 * levels), jnp.float32),
            pltpu.VMEM((size, size), jnp.bfloat16),
            pltpu.VMEM((size, size), jnp.bfloat16),
            pltpu.VMEM((2 * levels, 2 * levels), jnp.bfloat16),
        ],
        compiler_params=pltpu.CompilerParams(vmem_limit_bytes=40 * 2**20),
        name="microphysics",
    )(block_cost, state, level_mix, field_mix)


SIDES = ((-1, 0), (1, 0), (0, -1), (0, 1), (-1, -1), (-1, 1), (1, -1), (1, 1))


def dynamics_kernel(
    wide_count, narrow_count, chunks,
    state_ref, raw_ref, wind_x_ref, wind_y_ref, shift_ref,
    out_ref,
    div, row_out, row_in, col_out, col_in, tip_out, tip_in, send_sem, recv_sem,
):
    fields, rows, columns, levels = state_ref.shape
    wide = lax.axis_index("wide")
    narrow = lax.axis_index("narrow")
    ids = [
        {
            "wide": lax.rem(wide + dw + wide_count, wide_count),
            "narrow": lax.rem(narrow + dn + narrow_count, narrow_count),
        }
        for dw, dn in SIDES
    ]
    barrier = pltpu.get_barrier_semaphore()
    for device in ids:
        pl.semaphore_signal(barrier, inc=1, device_id=device, device_id_type=MESH)
    pl.semaphore_wait(barrier, len(SIDES))

    table = dyn_step * derivative_table()
    place = lax.broadcasted_iota(jnp.int32, (columns, levels), 0)
    at_right = (place % NP == NP - 1) & (place != columns - 1)
    at_left = (place % NP == 0) & (place != 0)
    is_edge = (place % NP == NP - 1) | (place % NP == 0)
    weight = jnp.where(is_edge, 0.5, 1.0).astype(jnp.float32)

    def paired(values):
        up = pltpu.roll(values, columns - 1, 0)
        down = pltpu.roll(values, 1, 0)
        return values + jnp.where(at_right, up, jnp.where(at_left, down, 0.0))

    def copies(step, chunk):
        lo, hi = chunks[chunk]
        span = pl.ds(lo, hi - lo)
        made = []
        for side, device in enumerate(ids):
            if side < 2:
                source, target = row_out.at[step, side, span], row_in.at[step, 1 - side, span]
            elif side < 4:
                source, target = col_out.at[step, side - 2, span], col_in.at[step, 3 - side, span]
            else:
                source, target = tip_out.at[step, side - 4, span], tip_in.at[step, 7 - side, span]
            made.append(pltpu.make_async_remote_copy(
                src_ref=source,
                dst_ref=target,
                send_sem=send_sem.at[step, chunk, side],
                recv_sem=recv_sem.at[step, chunk, side],
                device_id=device,
                device_id_type=MESH,
            ))
        return made

    def diverge(step, chunk, source_ref):
        lo, hi = chunks[chunk]

        def one_field(field, carry):
            for first in range(0, rows, NP):
                held = [source_ref[field, first + node] for node in range(NP)]
                flux_x = [
                    held[node] * wind_x_ref[first + node].astype(jnp.float32) for node in range(NP)
                ]
                for node in range(NP):
                    flux_y = held[node] * wind_y_ref[first + node].astype(jnp.float32)
                    flux_y = flux_y.reshape(columns // 8, 8, levels)
                    total = flux_y * shift_ref[0]
                    for shift in range(1, NP):
                        total = total + pltpu.roll(flux_y, 8 - shift, 1) * shift_ref[shift]
                        total = total + pltpu.roll(flux_y, shift, 1) * shift_ref[shift + NP - 1]
                    total = total.reshape(columns, levels)
                    for other in range(NP):
                        if table[node, other] != 0.0:
                            total = total + np.float32(table[node, other]) * flux_x[other]
                    div[field, first + node] = total
            row_out[step, 0, field] = div[field, 0]
            row_out[step, 1, field] = div[field, rows - 1]
            for end, column in enumerate((0, columns - 1)):
                col_out[step, end, field] = paired(div[field, :, column])
                tip_out[step, end, field] = div[field, 0, column:column + 1]
                tip_out[step, end + 2, field] = div[field, rows - 1, column:column + 1]
            return carry

        lax.fori_loop(lo, hi, one_field, 0)
        for copy in copies(step, chunk):
            copy.start()

    def advance(step, chunk, source_ref, tend_ref):
        lo, hi = chunks[chunk]
        for copy in copies(step, chunk):
            copy.wait_recv()

        def one_field(field, carry):
            for row in range(rows):
                total = div[field, row]
                low = col_in[step, 0, field, row:row + 1]
                high = col_in[step, 1, field, row:row + 1]
                if row == 0:
                    total = total + row_in[step, 0, field]
                    low = low + tip_in[step, 0, field]
                    high = high + tip_in[step, 1, field]
                elif row == rows - 1:
                    total = total + row_in[step, 1, field]
                    low = low + tip_in[step, 2, field]
                    high = high + tip_in[step, 3, field]
                elif row % NP == NP - 1:
                    total = total + div[field, row + 1]
                elif row % NP == 0:
                    total = total + div[field, row - 1]
                total = paired(total)
                total = total + jnp.where(place == 0, low, jnp.where(place == columns - 1, high, 0.0))
                scale = weight * 0.5 if row % NP in (0, NP - 1) else weight
                if tend_ref is None:
                    tend = dyn_step
                else:
                    tend = np.float32(dyn_step) * tend_ref[field, row]
                if source_ref is None:
                    start = 0.0
                else:
                    start = source_ref[field, row]
                out_ref[field, row] = start + (tend - scale * total)
            return carry

        lax.fori_loop(lo, hi, one_field, 0)

    last = fields
    out_ref[last] = jnp.full((rows, columns, levels), dyn_step, jnp.float32)

    field_chunks = [chunk for chunk, (lo, hi) in enumerate(chunks) if hi <= fields]
    unit_chunk = len(field_chunks)
    for chunk in field_chunks:
        diverge(0, chunk, state_ref)
    diverge(1, unit_chunk, out_ref)
    for chunk in field_chunks:
        advance(0, chunk, state_ref, raw_ref)
        diverge(1, chunk, out_ref)

    def substep(step, carry):
        for chunk in field_chunks:
            advance(step, chunk, out_ref, raw_ref)
            diverge(step + 1, chunk, out_ref)
        advance(step, unit_chunk, out_ref, None)
        diverge(step + 1, unit_chunk, out_ref)
        return carry

    lax.fori_loop(1, NSUB - 1, substep, 0)
    for chunk in field_chunks:
        advance(NSUB - 1, chunk, out_ref, raw_ref)
    advance(NSUB - 1, unit_chunk, out_ref, None)

    for step in range(NSUB):
        for chunk in range(len(chunks)):
            if step == 0 and chunk == unit_chunk:
                continue
            for copy in copies(step, chunk):
                copy.wait_send()


def dynamics(state, raw, wind_x, wind_y, wide_count, narrow_count):
    fields, rows, columns, levels = state.shape
    table = dyn_step * derivative_table()
    shifts = np.zeros((2 * NP - 1, 8, levels), np.float32)
    for place in range(8):
        node = place % NP
        shifts[0, place] = table[node, node]
        for shift in range(1, NP):
            if node + shift < NP:
                shifts[shift, place] = table[node, node + shift]
            if node - shift >= 0:
                shifts[shift + NP - 1, place] = table[node, node - shift]
    third = max(fields // 3, 1)
    cuts = list(range(0, fields, third)) + [fields]
    chunks = list(zip(cuts[:-1], cuts[1:])) + [(fields, fields + 1)]
    vmem = pl.BlockSpec(memory_space=pltpu.VMEM)
    count = fields + 1
    row_buffer = pltpu.VMEM((NSUB, 2, count, columns, levels), jnp.float32)
    col_buffer = pltpu.VMEM((NSUB, 2, count, rows, levels), jnp.float32)
    tip_buffer = pltpu.VMEM((NSUB, 4, count, 1, levels), jnp.float32)
    sems = pltpu.SemaphoreType.DMA((NSUB, len(chunks), len(SIDES)))
    return pl.pallas_call(
        functools.partial(dynamics_kernel, wide_count, narrow_count, chunks),
        out_shape=jax.ShapeDtypeStruct((count, rows, columns, levels), jnp.float32),
        in_specs=[vmem] * 5,
        out_specs=vmem,
        scratch_shapes=[
            pltpu.VMEM((count, rows, columns, levels), jnp.float32),
            row_buffer, row_buffer, col_buffer, col_buffer, tip_buffer, tip_buffer,
            sems, sems,
        ],
        compiler_params=pltpu.CompilerParams(
            collective_id=0, has_side_effects=True, vmem_limit_bytes=48 * 2**20
        ),
        cost_estimate=pl.CostEstimate(flops=10**8, bytes_accessed=6 * 10**7, transcendentals=0),
        name="dynamics",
    )(state, raw, wind_x, wind_y, jnp.asarray(shifts))


def per_device(state, wind_x, wind_y, level_mix, field_mix, block_cost):
    fields, rows, columns, levels = state.shape
    wide_count = lax.axis_size("wide")
    narrow_count = lax.axis_size("narrow")
    raw, partial_sum = microphysics(state, level_mix, field_mix, block_cost)
    total_sum = lax.psum(partial_sum, ("wide", "narrow"))
    mean = (total_sum / (rows * columns * wide_count * narrow_count))[:, None, None, :]
    moved = dynamics(state, raw, wind_x, wind_y, wide_count, narrow_count)
    return (moved[:fields] - mean * moved[fields:], raw - mean)


def solution(mesh):
    placed = (
        P(None, "wide", "narrow", None),
        P("wide", "narrow", None),
        P("wide", "narrow", None),
        P(),
        P(),
        P("wide", "narrow"),
    )
    return jax.shard_map(
        per_device,
        mesh=mesh,
        in_specs=placed,
        out_specs=(P(None, "wide", "narrow", None), P(None, "wide", "narrow", None)),
        check_vma=False,
    )
```

profile of v0, /device:TPU:0, one launch (start us, length us, event | category | flops | bytes accessed | tf_op | source)
XLA Modules:
  0.0 110.2 jit_solution(1896637872731754093)
XLA Ops:
  0.6 0.7 copy.9.cost_ref
  1.4 0.0 copy-start
  1.4 1.4 %copy-done = f32[12,16,16,128]{3,2,1,0:T(8,128)S(1)} copy-done((f32[12,16,16,128]{3,2,1,0:T(8,128)S(1)}, f32[12,16,16,128]{3,2,1,0:T(8,128)}, u32[]{:S(2)}) %copy-start) | copy-done | bytes 1572888
  2.8 0.0 copy-start.4
  2.8 0.8 copy-done.4
  3.5 0.0 copy-start.6
  3.5 0.7 copy-done.6
  4.2 0.0 copy-start.1
  4.2 0.0 copy-start.2
  4.2 10.0 %microphysics.1 = (f32[12,16,16,128]{3,2,1,0:T(8,128)S(1)}, f32[12,128]{1,0:T(8,128)S(1)}) custom-call(s32[2,1]{1,0:T(2,128)S(1)} %copy.9.cost_ref, f32[12,16,16,128]{3,2,1,0:T(8,128)S(1)} %copy-done, bf16[128,128]{1,0:T(8,128)(2,1)S(1)} %copy-done.4, f32[12,12]{1,0:T(8,128)S(1)} %copy-done.6), custom_call_target="tpu_custom_call" | custom-call | tf_op jit(solution)/shard_map/microphysics/pallas_call | solution.py:112
  14.3 58.9 %psum.7 = f32[12,128]{1,0:T(8,128)S(1)} all-reduce(f32[12,128]{1,0:T(8,128)S(1)} %get-tuple-element.5), channel_id=1, replica_groups=mesh['wide'=8,'narrow'=4] {'wide','narrow'}, use_global_device_ids=true, to_apply=%region_0.0 | all-reduce | flops 1536 | bytes 12288 | tf_op jit(solution)/shard_map/psum | solution.py:336
  73.1 0.0 copy-done.1
  73.2 0.0 copy-done.2
  73.2 0.0 copy-start.3
  73.2 0.8 copy-done.3
  74.0 0.0 copy-start.5
  74.0 0.7 copy-done.5
  74.7 33.5 %dynamics.1 = f32[13,16,16,128]{3,2,1,0:T(8,128)S(1)} custom-call(f32[12,16,16,128]{3,2,1,0:T(8,128)S(1)} %copy-done.1, f32[12,16,16,128]{3,2,1,0:T(8,128)S(1)} %get-tuple-element.4.raw_ref, bf16[16,16,128]{2,1,0:T(8,128)(2,1)S(1)} %copy-done.2, bf16[16,16,128]{2,1,0:T(8,128)(2,1)S(1)} %copy-done.3, f32[7,8,128]{2,1,0:T(8,128)S(1)} %copy-done.5), custom_call_target="tpu_custom_call" | custom-call | flops 100000000 | bytes 60000000 | tf_op jit(solution)/shard_map/dynamics/pallas_call | solution.py:313
  108.3 2.0 %broadcast_subtract_fusion = (f32[12,16,16,128]{3,2,1,0:T(8,128)}, f32[12,16,16,128]{3,2,1,0:T(8,128)}) fusion(f32[12,16,16,128]{3,2,1,0:T(8,128)S(1)} %get-tuple-element.4.raw_ref, f32[12,128]{1,0:T(8,128)S(1)} %broadcast_multiply_fusion, f32[16,16,128]{2,1,0:T(8,128)S(1)} %slice_bitcast_fusion, f32[13,16,16,128]{3,2,1,0:T(8,128)S(1)} %dynamics.1), kind=kLoop, calls=%fused_computation.1 | loop fusion | flops 1179648 | bytes 6428672 | tf_op jit(solution)/shard_map/sub | solution.py:339
  (2 shorter events, 0.0 us)
Async XLA Ops:
  1.4 1.4 %copy-start = (f32[12,16,16,128]{3,2,1,0:T(8,128)S(1)}, f32[12,16,16,128]{3,2,1,0:T(8,128)}, u32[]{:S(2)}) copy-start(f32[12,16,16,128]{3,2,1,0:T(8,128)} %state_ref.3) | copy-start | bytes 4718596
  2.8 0.8 copy-start.4
  3.5 0.7 copy-start.6
  4.2 68.9 %copy-start.1 = (f32[12,16,16,128]{3,2,1,0:T(8,128)S(1)}, f32[12,16,16,128]{3,2,1,0:T(8,128)}, u32[]{:S(2)}) copy-start(f32[12,16,16,128]{3,2,1,0:T(8,128)} %state_ref.3) | copy-start | bytes 4718596
  4.2 68.9 %copy-start.2 = (bf16[16,16,128]{2,1,0:T(8,128)(2,1)S(1)}, bf16[16,16,128]{2,1,0:T(8,128)(2,1)}, u32[]{:S(2)}) copy-start(bf16[16,16,128]{2,1,0:T(8,128)(2,1)} %wind_x_ref.1) | copy-start | bytes 196612
  73.2 0.8 copy-start.3
  74.0 0.7 copy-start.5
where the time goes:
time: 110 us
  blocking collectives  58.9 us (54%)
  Pallas kernels  43.5 us (40%)
  local copies, waits for them, and re-layouts  5.2 us (5%)
  other arithmetic  1.96 us (2%)
    psum x1, blocking collectives, per_device(): total_sum = lax.psum(partial_sum, ('wide', 'narrow'))  58.9 us
    pallas_call x1, Pallas kernels, dynamics(): pl.pallas_call(functools.partial(dynamics_kernel, wide_count, narrow_coun...  33.5 us
    pallas_call x1, Pallas kernels, microphysics(): pl.pallas_call(micro_kernel, out_shape=(jax.ShapeDtypeStruct(state.shape,...  10 us
    unnamed x15, local copies, waits for them, and re-layouts  5.19 us

commit v1 on v0

v1 whole, which is shorter than its diff:
```python
import functools
import math

import numpy as np
import jax
import jax.numpy as jnp
from jax import lax
from jax.experimental import pallas as pl
from jax.experimental.pallas import tpu as pltpu
from jax.sharding import PartitionSpec as P

NP = 4
NSUB = 4
MAXC = 24
BR = 8
MESH = pl.DeviceIdType.MESH

dyn_step = 0.05


def derivative_table():
    inner = 1.0 / math.sqrt(5.0)
    nodes = np.array([-1.0, -inner, inner, 1.0])
    identity = np.eye(4)
    spacing = nodes[:, None] - nodes[None, :] + identity
    barycentric = 1.0 / np.prod(spacing, axis=1)
    off_diag = barycentric[None, :] / barycentric[:, None] / spacing * (1.0 - identity)
    table = off_diag - identity * np.sum(off_diag, axis=1)[:, None]
    table[np.abs(table) < 1e-12] = 0.0
    return table


SIDES = ((-1, 0), (1, 0), (0, -1), (0, 1), (-1, -1), (-1, 1), (1, -1), (1, 1))


def doubling_steps(wide_count, narrow_count):
    steps = []
    for axis, count in (("narrow", narrow_count), ("wide", wide_count)):
        stride = 1
        while stride < count:
            steps.append((axis, stride))
            stride *= 2
    return steps


def whole_kernel(
    wide_count, narrow_count, chunks,
    cost_ref, state_hbm, wind_x_hbm, wind_y_hbm, level_hbm, field_hbm, shift_hbm,
    moved_hbm, raw_hbm, unit_hbm, sum_ref,
    state, wind_x, wind_y, level_in, field_in, shift_ref,
    raw_ref, out_ref, div, work, mix_hi, mix_lo, levels2,
    row_out, row_in, col_out, col_in, tip_out, tip_in, sum_out, sum_in,
    send_sem, recv_sem, sum_send, sum_recv, load_sem, store_sem,
):
    fields, rows, columns, levels = state.shape
    size = fields * columns
    count_blocks = rows // BR
    half = BR // 2
    wide = lax.axis_index("wide")
    narrow = lax.axis_index("narrow")
    ids = [
        {
            "wide": lax.rem(wide + dw + wide_count, wide_count),
            "narrow": lax.rem(narrow + dn + narrow_count, narrow_count),
        }
        for dw, dn in SIDES
    ]
    sum_ids = []
    for axis, stride in doubling_steps(wide_count, narrow_count):
        place_on = {"wide": wide, "narrow": narrow}
        mine = place_on[axis]
        place_on[axis] = mine + stride * (1 - 2 * lax.rem(mine // stride, 2))
        sum_ids.append(place_on)

    loads = [
        pltpu.make_async_copy(source, target, load_sem.at[index])
        for index, (source, target) in enumerate((
            (state_hbm, state), (wind_x_hbm, wind_x), (wind_y_hbm, wind_y),
            (shift_hbm, shift_ref), (field_hbm, field_in), (level_hbm, level_in),
        ))
    ]
    for load in loads:
        load.start()
    barrier = pltpu.get_barrier_semaphore()
    for device in ids + sum_ids:
        pl.semaphore_signal(barrier, inc=1, device_id=device, device_id_type=MESH)

    loads[4].wait()
    mix = field_in[...]
    high = mix.astype(jnp.bfloat16)
    low = (mix - high.astype(jnp.float32)).astype(jnp.bfloat16)
    wide_row = lax.broadcasted_iota(jnp.int32, (size, fields), 0) // columns
    spread = (wide_row == lax.broadcasted_iota(jnp.int32, (size, fields), 1)).astype(jnp.float32).astype(jnp.bfloat16)
    wide_col = lax.broadcasted_iota(jnp.int32, (fields, size), 1) // columns
    spread_t = (wide_col == lax.broadcasted_iota(jnp.int32, (fields, size), 0)).astype(jnp.float32).astype(jnp.bfloat16)
    same = (
        lax.broadcasted_iota(jnp.int32, (size, size), 0) % columns
        == lax.broadcasted_iota(jnp.int32, (size, size), 1) % columns
    )
    for part, held in ((high, mix_hi), (low, mix_lo)):
        tall = jnp.dot(spread, part, preferred_element_type=jnp.float32).astype(jnp.bfloat16)
        full = jnp.dot(tall, spread_t, preferred_element_type=jnp.float32)
        held[...] = jnp.where(same, full, 0.0).astype(jnp.bfloat16)
    loads[5].wait()
    levels2[...] = jnp.zeros_like(levels2)
    levels2[:levels, :levels] = level_in[...]
    levels2[levels:, levels:] = level_in[...]

    table = dyn_step * derivative_table()
    place = lax.broadcasted_iota(jnp.int32, (columns, levels), 0)
    at_right = (place % NP == NP - 1) & (place != columns - 1)
    at_left = (place % NP == 0) & (place != 0)
    is_edge = (place % NP == NP - 1) | (place % NP == 0)
    weight = jnp.where(is_edge, 0.5, 1.0).astype(jnp.float32)

    def paired(values):
        up = pltpu.roll(values, columns - 1, 0)
        down = pltpu.roll(values, 1, 0)
        return values + jnp.where(at_right, up, jnp.where(at_left, down, 0.0))

    def copies(step, chunk):
        lo, hi = chunks[chunk]
        span = pl.ds(lo, hi - lo)
        made = []
        for side, device in enumerate(ids):
            if side < 2:
                source, target = row_out.at[step, side, span], row_in.at[step, 1 - side, span]
            elif side < 4:
                source, target = col_out.at[step, side - 2, span], col_in.at[step, 3 - side, span]
            else:
                source, target = tip_out.at[step, side - 4, span], tip_in.at[step, 7 - side, span]
            made.append(pltpu.make_async_remote_copy(
                src_ref=source,
                dst_ref=target,
                send_sem=send_sem.at[step, chunk, side],
                recv_sem=recv_sem.at[step, chunk, side],
                device_id=device,
                device_id_type=MESH,
            ))
        return made

    def sum_copy(index):
        return pltpu.make_async_remote_copy(
            src_ref=sum_out.at[index],
            dst_ref=sum_in.at[index],
            send_sem=sum_send.at[index],
            recv_sem=sum_recv.at[index],
            device_id=sum_ids[index],
            device_id_type=MESH,
        )

    def add_sum(index):
        sum_copy(index).wait_recv()
        total = sum_out[index] + sum_in[index]
        if index + 1 < len(sum_ids):
            sum_out[index + 1] = total
            sum_copy(index + 1).start()
        else:
            sum_ref[...] = total

    def diverge(step, chunk, source_ref):
        lo, hi = chunks[chunk]

        def one_field(field, carry):
            for first in range(0, rows, NP):
                held = [source_ref[field, first + node] for node in range(NP)]
                flux_x = [
                    held[node] * wind_x[first + node].astype(jnp.float32) for node in range(NP)
                ]
                for node in range(NP):
                    flux_y = held[node] * wind_y[first + node].astype(jnp.float32)
                    flux_y = flux_y.reshape(columns // 8, 8, levels)
                    total = flux_y * shift_ref[0]
                    for shift in range(1, NP):
                        total = total + pltpu.roll(flux_y, 8 - shift, 1) * shift_ref[shift]
                        total = total + pltpu.roll(flux_y, shift, 1) * shift_ref[shift + NP - 1]
                    total = total.reshape(columns, levels)
                    for other in range(NP):
                        if table[node, other] != 0.0:
                            total = total + np.float32(table[node, other]) * flux_x[other]
                    div[field, first + node] = total
            row_out[step, 0, field] = div[field, 0]
            row_out[step, 1, field] = div[field, rows - 1]
            for end, column in enumerate((0, columns - 1)):
                col_out[step, end, field] = paired(div[field, :, column])
                tip_out[step, end, field] = div[field, 0, column:column + 1]
                tip_out[step, end + 2, field] = div[field, rows - 1, column:column + 1]
            return carry

        lax.fori_loop(lo, hi, one_field, 0)
        for copy in copies(step, chunk):
            copy.start()

    def advance(step, chunk, source_ref, tend_of):
        lo, hi = chunks[chunk]
        for copy in copies(step, chunk):
            copy.wait_recv()

        def one_field(field, carry):
            for row in range(rows):
                total = div[field, row]
                low = col_in[step, 0, field, row:row + 1]
                high = col_in[step, 1, field, row:row + 1]
                if row == 0:
                    total = total + row_in[step, 0, field]
                    low = low + tip_in[step, 0, field]
                    high = high + tip_in[step, 1, field]
                elif row == rows - 1:
                    total = total + row_in[step, 1, field]
                    low = low + tip_in[step, 2, field]
                    high = high + tip_in[step, 3, field]
                elif row % NP == NP - 1:
                    total = total + div[field, row + 1]
                elif row % NP == 0:
                    total = total + div[field, row - 1]
                total = paired(total)
                total = total + jnp.where(place == 0, low, jnp.where(place == columns - 1, high, 0.0))
                scale = weight * 0.5 if row % NP in (0, NP - 1) else weight
                out_ref[field, row] = source_ref[field, row] + (tend_of(field, row) - scale * total)
            return carry

        lax.fori_loop(lo, hi, one_field, 0)

    def of_raw(field, row):
        return np.float32(dyn_step) * raw_ref[field, row]

    last = fields
    unit_chunk = len(chunks) - 1
    field_chunks = range(unit_chunk)
    out_ref[last] = jnp.full((rows, columns, levels), dyn_step, jnp.float32)
    for load in loads[:4]:
        load.wait()
    pl.semaphore_wait(barrier, len(ids) + len(sum_ids))
    diverge(1, unit_chunk, out_ref)
    for chunk in field_chunks:
        diverge(0, chunk, state)

    parts = [
        (block, group, side, block * BR + side * half + group)
        for block in range(count_blocks) for group in range(half) for side in range(2)
    ]
    for block, group, side, row in parts:
        work[block, group, :, side * levels:(side + 1) * levels] = state[:, row].reshape(size, levels)

    counts = [cost_ref[block, 0] for block in range(count_blocks)]

    def turns(index, carry):
        for block in range(count_blocks):
            gain = jnp.where(index < counts[block], 0.5, 0.0).astype(jnp.float32)
            keep = 1.0 - gain
            for group in range(half):
                current = work[block, group]
                rounded = current.astype(jnp.bfloat16)
                coupled = jnp.dot(mix_hi[...], rounded, preferred_element_type=jnp.float32)
                coupled = coupled + jnp.dot(mix_lo[...], rounded, preferred_element_type=jnp.float32)
                mixed = jnp.dot(coupled.astype(jnp.bfloat16), levels2[...], preferred_element_type=jnp.float32)
                work[block, group] = keep * current + gain * jnp.tanh(mixed)
        return carry

    cuts = [MAXC * part // NSUB for part in range(NSUB + 1)]
    for part in range(NSUB):
        lax.fori_loop(cuts[part], cuts[part + 1], turns, 0)
        if part == 0:
            for chunk in field_chunks:
                advance(0, chunk, state, lambda field, row: 0.0)
        else:
            advance(part, unit_chunk, out_ref, lambda field, row: np.float32(dyn_step))
            if part < NSUB - 1:
                diverge(part + 1, unit_chunk, out_ref)
    unit_store = pltpu.make_async_copy(out_ref.at[last], unit_hbm, store_sem.at[0])
    unit_store.start()

    stores = []

    def store(source_ref, target_ref, chunk):
        lo, hi = chunks[chunk]
        span = pl.ds(lo, hi - lo)
        stores.append(pltpu.make_async_copy(source_ref.at[span], target_ref.at[span], store_sem.at[len(stores) + 1]))
        stores[-1].start()

    for chunk in field_chunks:
        def end_field(field, carry):
            total = jnp.zeros((columns, levels), jnp.float32)
            here = pl.ds(pl.multiple_of(field * columns, columns), columns)
            for block, group, side, row in parts:
                ended = work[block, group, here, side * levels:(side + 1) * levels]
                raw = ended - state[field, row]
                raw_ref[field, row] = raw
                out_ref[field, row] = out_ref[field, row] + np.float32(dyn_step) * raw
                total = total + raw
            sum_out[0, field] = jnp.sum(total, axis=0, keepdims=True)
            return carry

        lax.fori_loop(chunks[chunk][0], chunks[chunk][1], end_field, 0)
        diverge(1, chunk, out_ref)
        store(raw_ref, raw_hbm, chunk)
    sum_copy(0).start()

    sums_left = list(range(len(sum_ids)))
    for step in range(1, NSUB):
        for chunk in field_chunks:
            advance(step, chunk, out_ref, of_raw)
            if step < NSUB - 1:
                diverge(step + 1, chunk, out_ref)
            else:
                store(out_ref, moved_hbm, chunk)
            if sums_left and not (step == 1 and chunk == 0):
                add_sum(sums_left.pop(0))
    for index in sums_left:
        add_sum(index)

    for step in range(NSUB):
        for chunk in range(len(chunks)):
            if step == 0 and chunk == unit_chunk:
                continue
            for copy in copies(step, chunk):
                copy.wait_send()
    for index in range(len(sum_ids)):
        sum_copy(index).wait_send()
    unit_store.wait()
    for made in stores:
        made.wait()


def whole(state, wind_x, wind_y, level_mix, field_mix, block_cost, wide_count, narrow_count):
    fields, rows, columns, levels = state.shape
    table = dyn_step * derivative_table()
    shifts = np.zeros((2 * NP - 1, 8, levels), np.float32)
    for place in range(8):
        node = place % NP
        shifts[0, place] = table[node, node]
        for shift in range(1, NP):
            if node + shift < NP:
                shifts[shift, place] = table[node, node + shift]
            if node - shift >= 0:
                shifts[shift + NP - 1, place] = table[node, node - shift]
    third = max(fields // 3, 1)
    cuts = list(range(0, fields, third)) + [fields]
    chunks = list(zip(cuts[:-1], cuts[1:])) + [(fields, fields + 1)]
    vmem = pl.BlockSpec(memory_space=pltpu.VMEM)
    hbm = pl.BlockSpec(memory_space=pl.ANY)
    count = fields + 1
    size = fields * columns
    row_buffer = pltpu.VMEM((NSUB, 2, count, columns, levels), jnp.float32)
    col_buffer = pltpu.VMEM((NSUB, 2, count, rows, levels), jnp.float32)
    tip_buffer = pltpu.VMEM((NSUB, 4, count, 1, levels), jnp.float32)
    sems = pltpu.SemaphoreType.DMA((NSUB, len(chunks), len(SIDES)))
    steps = len(doubling_steps(wide_count, narrow_count))
    sum_buffer = pltpu.VMEM((steps, fields, 1, levels), jnp.float32)
    field_buffer = pltpu.VMEM(state.shape, jnp.float32)
    count_buffer = pltpu.VMEM((count, rows, columns, levels), jnp.float32)
    return pl.pallas_call(
        functools.partial(whole_kernel, wide_count, narrow_count, chunks),
        out_shape=(
            jax.ShapeDtypeStruct(state.shape, jnp.float32),
            jax.ShapeDtypeStruct(state.shape, jnp.float32),
            jax.ShapeDtypeStruct((rows, columns, levels), jnp.float32),
            jax.ShapeDtypeStruct((fields, 1, levels), jnp.float32),
        ),
        in_specs=[pl.BlockSpec(memory_space=pltpu.SMEM)] + [hbm] * 6,
        out_specs=(hbm, hbm, hbm, vmem),
        scratch_shapes=[
            field_buffer,
            pltpu.VMEM(wind_x.shape, wind_x.dtype),
            pltpu.VMEM(wind_y.shape, wind_y.dtype),
            pltpu.VMEM(level_mix.shape, level_mix.dtype),
            pltpu.VMEM(field_mix.shape, field_mix.dtype),
            pltpu.VMEM(shifts.shape, jnp.float32),
            field_buffer, count_buffer, count_buffer,
            pltpu.VMEM((rows // BR, BR // 2, size, 2 * levels), jnp.float32),
            pltpu.VMEM((size, size), jnp.bfloat16),
            pltpu.VMEM((size, size), jnp.bfloat16),
            pltpu.VMEM((2 * levels, 2 * levels), jnp.bfloat16),
            row_buffer, row_buffer, col_buffer, col_buffer, tip_buffer, tip_buffer,
            sum_buffer, sum_buffer,
            sems, sems,
            pltpu.SemaphoreType.DMA((steps,)),
            pltpu.SemaphoreType.DMA((steps,)),
            pltpu.SemaphoreType.DMA((6,)),
            pltpu.SemaphoreType.DMA((2 * len(chunks),)),
        ],
        compiler_params=pltpu.CompilerParams(
            collective_id=0, has_side_effects=True, vmem_limit_bytes=48 * 2**20
        ),
        cost_estimate=pl.CostEstimate(flops=10**9, bytes_accessed=6 * 10**7, transcendentals=10**7),
        name="columns_and_transport",
    )(block_cost, state, wind_x, wind_y, level_mix, field_mix, jnp.asarray(shifts))


def per_device(state, wind_x, wind_y, level_mix, field_mix, block_cost):
    fields, rows, columns, levels = state.shape
    wide_count = lax.axis_size("wide")
    narrow_count = lax.axis_size("narrow")
    moved, raw, unit, total = whole(
        state, wind_x, wind_y, level_mix, field_mix, block_cost, wide_count, narrow_count
    )
    mean = (total / (rows * columns * wide_count * narrow_count))[:, :, None, :]
    return (moved - mean * unit[None], raw - mean)


def solution(mesh):
    placed = (
        P(None, "wide", "narrow", None),
        P("wide", "narrow", None),
        P("wide", "narrow", None),
        P(),
        P(),
        P("wide", "narrow"),
    )
    return jax.shard_map(
        per_device,
        mesh=mesh,
        in_specs=placed,
        out_specs=(P(None, "wide", "narrow", None), P(None, "wide", "narrow", None)),
        check_vma=False,
    )
```

time: 110 us -> 90.1 us (0.82)
  blocking collectives: 58.9 us -> 0 us
  Pallas kernels: 43.5 us -> 81 us
    psum x1 -> x0, blocking collectives: 58.9 us -> none  [per_device(): total_sum = lax.psum(partial_sum, ('wide', 'narrow'))]
    pallas_call x2 -> x1, Pallas kernels: 43.5 us -> 81 us  [whole(): pl.pallas_call(functools.partial(whole_kernel, wide_count, narrow_count,...]
    unnamed x15 -> x14, local copies, waits for them, and re-layouts: 5.19 us -> 6.03 us
where the time goes in v1:
time: 90.1 us; the launch traced here: 89.7 us
  Pallas kernels  81 us (90%)
  local copies, waits for them, and re-layouts  6.03 us (7%)
  other arithmetic  1.97 us (2%)
    pallas_call x1, Pallas kernels, whole(): pl.pallas_call(functools.partial(whole_kernel, wide_count, narrow_count,...  81 us
    unnamed x14, local copies, waits for them, and re-layouts  6.03 us
    sub x1, other arithmetic, per_device(): return (moved - mean * unit[None], raw - mean)  1.96 us

profile of v1, /device:TPU:0, one launch (start us, length us, event | category | flops | bytes accessed | tf_op | source)
XLA Modules:
  0.0 89.7 jit_solution(13358336966517063034)
XLA Ops:
  0.6 0.7 copy.9.cost_ref
  1.4 0.0 copy-start
  1.4 1.4 %copy-done = f32[12,16,16,128]{3,2,1,0:T(8,128)S(1)} copy-done((f32[12,16,16,128]{3,2,1,0:T(8,128)S(1)}, f32[12,16,16,128]{3,2,1,0:T(8,128)}, u32[]{:S(2)}) %copy-start) | copy-done | bytes 1572888
  2.8 0.0 copy-start.1
  2.8 0.8 copy-done.1
  3.6 0.0 copy-start.2
  3.6 0.8 copy-done.2
  4.5 0.0 copy-start.3
  4.5 0.8 copy-done.3
  5.2 0.0 copy-start.4
  5.2 0.7 copy-done.4
  5.9 0.0 copy-start.5
  5.9 0.7 copy-done.5
  6.7 81.0 %columns_and_transport.1 = (f32[12,16,16,128]{3,2,1,0:T(8,128)S(1)}, f32[12,16,16,128]{3,2,1,0:T(8,128)S(1)}, f32[16,16,128]{2,1,0:T(8,128)S(1)}, f32[12,1,128]{2,1,0:T(1,128)S(1)}) custom-call(s32[2,1]{1,0:T(2,128)S(1)} %copy.9.cost_ref, f32[12,16,16,128]{3,2,1,0:T(8,128)S(1)} %copy-done, bf16[16,16,128]{2,1,0:T(8,128)(2,1)S(1)} %copy-done.1, ...), custom_call_target="tpu_custom_call" | custom-call | flops 1000000000 | bytes 60000000 | tf_op jit(solution)/shard_map/columns_and_transport/pallas_call | solution.py:352
  87.7 2.0 %broadcast_subtract_fusion = (f32[12,16,16,128]{3,2,1,0:T(8,128)}, f32[12,16,16,128]{3,2,1,0:T(8,128)}) fusion(f32[12,16,16,128]{3,2,1,0:T(8,128)S(1)} %get-tuple-element.9, f32[12,128]{1,0:T(8,128)S(1)} %bitcast.3, f32[12,16,16,128]{3,2,1,0:T(8,128)S(1)} %get-tuple-element.6, f32[16,16,128]{2,1,0:T(8,128)S(1)} %get-tuple-element.8), kind=kLoop, calls=%fused_computation.1 | loop fusion | flops 1179648 | bytes 6428672 | tf_op jit(solution)/shard_map/sub | solution.py:398
  (2 shorter events, 0.0 us)
Async XLA Ops:
  1.4 1.4 %copy-start = (f32[12,16,16,128]{3,2,1,0:T(8,128)S(1)}, f32[12,16,16,128]{3,2,1,0:T(8,128)}, u32[]{:S(2)}) copy-start(f32[12,16,16,128]{3,2,1,0:T(8,128)} %state_hbm.1) | copy-start | bytes 4718596
  2.8 0.8 copy-start.1
  3.6 0.8 copy-start.2
  4.5 0.8 copy-start.3
  5.2 0.7 copy-start.4
  5.9 0.7 copy-start.5

commit v2 on v1

--- a/solution.py
+++ b/solution.py
@@ -45,10 +45,10 @@
 
 def whole_kernel(
     wide_count, narrow_count, chunks,
-    cost_ref, state_hbm, wind_x_hbm, wind_y_hbm, level_hbm, field_hbm, shift_hbm,
-    moved_hbm, raw_hbm, unit_hbm, sum_ref,
-    state, wind_x, wind_y, level_in, field_in, shift_ref,
-    raw_ref, out_ref, div, work, mix_hi, mix_lo, levels2,
+    cost_ref, state_hbm, wind_x_hbm, wind_y_hbm, level_hbm, field_hbm,
+    out_hbm, raw_hbm, sum_ref,
+    out_ref, raw_ref, state, wind_x_in, wind_y_in, level_in, field_in, wind_x, wind_y, shift_ref,
+    div, work, coupled_ref, mixer, levels2,
     row_out, row_in, col_out, col_in, tip_out, tip_in, sum_out, sum_in,
     send_sem, recv_sem, sum_send, sum_recv, load_sem, store_sem,
 ):
@@ -75,8 +75,8 @@
     loads = [
         pltpu.make_async_copy(source, target, load_sem.at[index])
         for index, (source, target) in enumerate((
-            (state_hbm, state), (wind_x_hbm, wind_x), (wind_y_hbm, wind_y),
-            (shift_hbm, shift_ref), (field_hbm, field_in), (level_hbm, level_in),
+            (field_hbm, field_in), (level_hbm, level_in),
+            (wind_x_hbm, wind_x_in), (wind_y_hbm, wind_y_in), (state_hbm, state),
         ))
     ]
     for load in loads:
@@ -85,7 +85,7 @@
     for device in ids + sum_ids:
         pl.semaphore_signal(barrier, inc=1, device_id=device, device_id_type=MESH)
 
-    loads[4].wait()
+    loads[0].wait()
     mix = field_in[...]
     high = mix.astype(jnp.bfloat16)
     low = (mix - high.astype(jnp.float32)).astype(jnp.bfloat16)
@@ -97,16 +97,25 @@
         lax.broadcasted_iota(jnp.int32, (size, size), 0) % columns
         == lax.broadcasted_iota(jnp.int32, (size, size), 1) % columns
     )
-    for part, held in ((high, mix_hi), (low, mix_lo)):
+    for index, part in enumerate((high, low)):
         tall = jnp.dot(spread, part, preferred_element_type=jnp.float32).astype(jnp.bfloat16)
         full = jnp.dot(tall, spread_t, preferred_element_type=jnp.float32)
-        held[...] = jnp.where(same, full, 0.0).astype(jnp.bfloat16)
-    loads[5].wait()
+        mixer[index * size:(index + 1) * size] = jnp.where(same, full, 0.0).astype(jnp.bfloat16)
+    loads[1].wait()
     levels2[...] = jnp.zeros_like(levels2)
     levels2[:levels, :levels] = level_in[...]
     levels2[levels:, levels:] = level_in[...]
 
     table = dyn_step * derivative_table()
+    tile_place = lax.broadcasted_iota(jnp.int32, (8, levels), 0)
+    node_place = tile_place % NP
+    for shift in range(1 - NP, NP):
+        value = jnp.zeros((8, levels), jnp.float32)
+        for node in range(NP):
+            if 0 <= node + shift < NP:
+                value = jnp.where(node_place == node, np.float32(table[node, node + shift]), value)
+        shift_ref[shift if shift >= 0 else NP - 1 - shift] = value
+
     place = lax.broadcasted_iota(jnp.int32, (columns, levels), 0)
     at_right = (place % NP == NP - 1) & (place != columns - 1)
     at_left = (place % NP == 0) & (place != 0)
@@ -118,11 +127,28 @@
         down = pltpu.roll(values, 1, 0)
         return values + jnp.where(at_right, up, jnp.where(at_left, down, 0.0))
 
+    def joined(values, low, high):
+        count = columns // 8
+        tiles = [values[8 * tile:8 * tile + 8] for tile in range(count)]
+        ups = [pltpu.roll(tile, 7, 0) for tile in tiles]
+        downs = [pltpu.roll(tile, 1, 0) for tile in tiles]
+        result = []
+        for tile in range(count):
+            before = downs[tile - 1] if tile else low
+            after = ups[tile + 1] if tile + 1 < count else high
+            other = jnp.where(tile_place == 7, after, 0.0)
+            other = jnp.where(tile_place == 0, before, other)
+            other = jnp.where(tile_place == 3, ups[tile], other)
+            other = jnp.where(tile_place == 4, downs[tile], other)
+            result.append(tiles[tile] + other)
+        return jnp.concatenate(result, axis=0)
+
     def copies(step, chunk):
         lo, hi = chunks[chunk]
         span = pl.ds(lo, hi - lo)
         made = []
         for side, device in enumerate(ids):
+            kind = min(side // 2, 2)
             if side < 2:
                 source, target = row_out.at[step, side, span], row_in.at[step, 1 - side, span]
             elif side < 4:
@@ -132,12 +158,19 @@
             made.append(pltpu.make_async_remote_copy(
                 src_ref=source,
                 dst_ref=target,
-                send_sem=send_sem.at[step, chunk, side],
-                recv_sem=recv_sem.at[step, chunk, side],
+                send_sem=send_sem.at[kind],
+                recv_sem=recv_sem.at[step, chunk, kind],
                 device_id=device,
                 device_id_type=MESH,
             ))
         return made
+
+    def arrive(step, chunk):
+        lo, hi = chunks[chunk]
+        span = pl.ds(lo, hi - lo)
+        for kind, held in enumerate((row_in, col_in, tip_in)):
+            here = held.at[step, :, span]
+            pltpu.make_async_copy(here, here, recv_sem.at[step, chunk, kind]).wait()
 
     def sum_copy(index):
         return pltpu.make_async_remote_copy(
@@ -158,17 +191,17 @@
         else:
             sum_ref[...] = total
 
-    def diverge(step, chunk, source_ref):
+    def diverge(step, chunk, source_ref, sends=True):
         lo, hi = chunks[chunk]
 
         def one_field(field, carry):
             for first in range(0, rows, NP):
                 held = [source_ref[field, first + node] for node in range(NP)]
                 flux_x = [
-                    held[node] * wind_x[first + node].astype(jnp.float32) for node in range(NP)
+                    held[node] * wind_x[first + node] for node in range(NP)
                 ]
                 for node in range(NP):
-                    flux_y = held[node] * wind_y[first + node].astype(jnp.float32)
+                    flux_y = held[node] * wind_y[first + node]
                     flux_y = flux_y.reshape(columns // 8, 8, levels)
                     total = flux_y * shift_ref[0]
                     for shift in range(1, NP):
@@ -188,13 +221,13 @@
             return carry
 
         lax.fori_loop(lo, hi, one_field, 0)
-        for copy in copies(step, chunk):
-            copy.start()
+        if sends:
+            for copy in copies(step, chunk):
+                copy.start()
 
     def advance(step, chunk, source_ref, tend_of):
         lo, hi = chunks[chunk]
-        for copy in copies(step, chunk):
-            copy.wait_recv()
+        arrive(step, chunk)
 
         def one_field(field, carry):
             for row in range(rows):
@@ -213,8 +246,7 @@
                     total = total + div[field, row + 1]
                 elif row % NP == 0:
                     total = total + div[field, row - 1]
-                total = paired(total)
-                total = total + jnp.where(place == 0, low, jnp.where(place == columns - 1, high, 0.0))
+                total = joined(total, low, high)
                 scale = weight * 0.5 if row % NP in (0, NP - 1) else weight
                 out_ref[field, row] = source_ref[field, row] + (tend_of(field, row) - scale * total)
             return carry
@@ -228,12 +260,19 @@
     unit_chunk = len(chunks) - 1
     field_chunks = range(unit_chunk)
     out_ref[last] = jnp.full((rows, columns, levels), dyn_step, jnp.float32)
-    for load in loads[:4]:
+    for load in loads[2:]:
         load.wait()
+    wind_x[...] = wind_x_in[...].astype(jnp.float32)
+    wind_y[...] = wind_y_in[...].astype(jnp.float32)
+    for chunk in field_chunks:
+        diverge(0, chunk, state, sends=False)
+    diverge(1, unit_chunk, out_ref, sends=False)
     pl.semaphore_wait(barrier, len(ids) + len(sum_ids))
-    diverge(1, unit_chunk, out_ref)
     for chunk in field_chunks:
-        diverge(0, chunk, state)
+        for copy in copies(0, chunk):
+            copy.start()
+    for copy in copies(1, unit_chunk):
+        copy.start()
 
     parts = [
         (block, group, side, block * BR + side * half + group)
@@ -242,24 +281,28 @@
     for block, group, side, row in parts:
         work[block, group, :, side * levels:(side + 1) * levels] = state[:, row].reshape(size, levels)
 
-    counts = [cost_ref[block, 0] for block in range(count_blocks)]
+    counts = [cost_ref[block] for block in range(count_blocks)]
 
     def turns(index, carry):
         for block in range(count_blocks):
             gain = jnp.where(index < counts[block], 0.5, 0.0).astype(jnp.float32)
             keep = 1.0 - gain
             for group in range(half):
-                current = work[block, group]
-                rounded = current.astype(jnp.bfloat16)
-                coupled = jnp.dot(mix_hi[...], rounded, preferred_element_type=jnp.float32)
-                coupled = coupled + jnp.dot(mix_lo[...], rounded, preferred_element_type=jnp.float32)
-                mixed = jnp.dot(coupled.astype(jnp.bfloat16), levels2[...], preferred_element_type=jnp.float32)
-                work[block, group] = keep * current + gain * jnp.tanh(mixed)
+                rounded = work[block, group].astype(jnp.bfloat16)
+                coupled = jnp.dot(mixer[...], rounded, preferred_element_type=jnp.float32)
+                coupled_ref[block, group * size:(group + 1) * size] = (
+                    coupled[:size] + coupled[size:]
+                ).astype(jnp.bfloat16)
+            mixed = jnp.dot(coupled_ref[block], levels2[...], preferred_element_type=jnp.float32)
+            for group in range(half):
+                work[block, group] = keep * work[block, group] + gain * jnp.tanh(
+                    mixed[group * size:(group + 1) * size]
+                )
         return carry
 
     cuts = [MAXC * part // NSUB for part in range(NSUB + 1)]
     for part in range(NSUB):
-        lax.fori_loop(cuts[part], cuts[part + 1], turns, 0)
+        lax.fori_loop(cuts[part], cuts[part + 1], turns, 0, unroll=3)
         if part == 0:
             for chunk in field_chunks:
                 advance(0, chunk, state, lambda field, row: 0.0)
@@ -267,17 +310,16 @@
             advance(part, unit_chunk, out_ref, lambda field, row: np.float32(dyn_step))
             if part < NSUB - 1:
                 diverge(part + 1, unit_chunk, out_ref)
-    unit_store = pltpu.make_async_copy(out_ref.at[last], unit_hbm, store_sem.at[0])
-    unit_store.start()
 
     stores = []
 
     def store(source_ref, target_ref, chunk):
         lo, hi = chunks[chunk]
         span = pl.ds(lo, hi - lo)
-        stores.append(pltpu.make_async_copy(source_ref.at[span], target_ref.at[span], store_sem.at[len(stores) + 1]))
+        stores.append(pltpu.make_async_copy(source_ref.at[span], target_ref.at[span], store_sem.at[len(stores)]))
         stores[-1].start()
 
+    store(out_ref, out_hbm, unit_chunk)
     for chunk in field_chunks:
         def end_field(field, carry):
             total = jnp.zeros((columns, levels), jnp.float32)
@@ -303,48 +345,33 @@
             if step < NSUB - 1:
                 diverge(step + 1, chunk, out_ref)
             else:
-                store(out_ref, moved_hbm, chunk)
+                store(out_ref, out_hbm, chunk)
             if sums_left and not (step == 1 and chunk == 0):
                 add_sum(sums_left.pop(0))
     for index in sums_left:
         add_sum(index)
 
-    for step in range(NSUB):
-        for chunk in range(len(chunks)):
-            if step == 0 and chunk == unit_chunk:
-                continue
-            for copy in copies(step, chunk):
-                copy.wait_send()
+    for kind, held in enumerate((row_out, col_out, tip_out)):
+        for here in (held.at[0, :, pl.ds(0, fields)], held.at[pl.ds(1, NSUB - 1)]):
+            pltpu.make_async_copy(here, here, send_sem.at[kind]).wait()
     for index in range(len(sum_ids)):
         sum_copy(index).wait_send()
-    unit_store.wait()
     for made in stores:
         made.wait()
 
 
 def whole(state, wind_x, wind_y, level_mix, field_mix, block_cost, wide_count, narrow_count):
     fields, rows, columns, levels = state.shape
-    table = dyn_step * derivative_table()
-    shifts = np.zeros((2 * NP - 1, 8, levels), np.float32)
-    for place in range(8):
-        node = place % NP
-        shifts[0, place] = table[node, node]
-        for shift in range(1, NP):
-            if node + shift < NP:
-                shifts[shift, place] = table[node, node + shift]
-            if node - shift >= 0:
-                shifts[shift + NP - 1, place] = table[node, node - shift]
     third = max(fields // 3, 1)
     cuts = list(range(0, fields, third)) + [fields]
     chunks = list(zip(cuts[:-1], cuts[1:])) + [(fields, fields + 1)]
     vmem = pl.BlockSpec(memory_space=pltpu.VMEM)
-    hbm = pl.BlockSpec(memory_space=pl.ANY)
+    hbm = pl.BlockSpec(memory_space=pltpu.HBM)
     count = fields + 1
     size = fields * columns
     row_buffer = pltpu.VMEM((NSUB, 2, count, columns, levels), jnp.float32)
     col_buffer = pltpu.VMEM((NSUB, 2, count, rows, levels), jnp.float32)
     tip_buffer = pltpu.VMEM((NSUB, 4, count, 1, levels), jnp.float32)
-    sems = pltpu.SemaphoreType.DMA((NSUB, len(chunks), len(SIDES)))
     steps = len(doubling_steps(wide_count, narrow_count))
     sum_buffer = pltpu.VMEM((steps, fields, 1, levels), jnp.float32)
     field_buffer = pltpu.VMEM(state.shape, jnp.float32)
@@ -352,50 +379,112 @@
     return pl.pallas_call(
         functools.partial(whole_kernel, wide_count, narrow_count, chunks),
         out_shape=(
+            jax.ShapeDtypeStruct((count, rows, columns, levels), jnp.float32),
             jax.ShapeDtypeStruct(state.shape, jnp.float32),
-            jax.ShapeDtypeStruct(state.shape, jnp.float32),
-            jax.ShapeDtypeStruct((rows, columns, levels), jnp.float32),
             jax.ShapeDtypeStruct((fields, 1, levels), jnp.float32),
         ),
-        in_specs=[pl.BlockSpec(memory_space=pltpu.SMEM)] + [hbm] * 6,
-        out_specs=(hbm, hbm, hbm, vmem),
+        in_specs=[pl.BlockSpec(memory_space=pltpu.SMEM)] + [hbm] * 5,
+        out_specs=(hbm, hbm, vmem),
         scratch_shapes=[
-            field_buffer,
+            count_buffer, field_buffer, field_buffer,
             pltpu.VMEM(wind_x.shape, wind_x.dtype),
             pltpu.VMEM(wind_y.shape, wind_y.dtype),
             pltpu.VMEM(level_mix.shape, level_mix.dtype),
             pltpu.VMEM(field_mix.shape, field_mix.dtype),
-            pltpu.VMEM(shifts.shape, jnp.float32),
-            field_buffer, count_buffer, count_buffer,
+            pltpu.VMEM(wind_x.shape, jnp.float32),
+            pltpu.VMEM(wind_y.shape, jnp.float32),
+            pltpu.VMEM((2 * NP - 1, 8, levels), jnp.float32),
+            count_buffer,
             pltpu.VMEM((rows // BR, BR // 2, size, 2 * levels), jnp.float32),
-            pltpu.VMEM((size, size), jnp.bfloat16),
-            pltpu.VMEM((size, size), jnp.bfloat16),
+            pltpu.VMEM((rows // BR, BR // 2 * size, 2 * levels), jnp.bfloat16),
+            pltpu.VMEM((2 * size, size), jnp.bfloat16),
             pltpu.VMEM((2 * levels, 2 * levels), jnp.bfloat16),
             row_buffer, row_buffer, col_buffer, col_buffer, tip_buffer, tip_buffer,
             sum_buffer, sum_buffer,
-            sems, sems,
+            pltpu.SemaphoreType.DMA((3,)),
+            pltpu.SemaphoreType.DMA((NSUB, len(chunks), 3)),
             pltpu.SemaphoreType.DMA((steps,)),
             pltpu.SemaphoreType.DMA((steps,)),
-            pltpu.SemaphoreType.DMA((6,)),
+            pltpu.SemaphoreType.DMA((5,)),
             pltpu.SemaphoreType.DMA((2 * len(chunks),)),
         ],
         compiler_params=pltpu.CompilerParams(
-            collective_id=0, has_side_effects=True, vmem_limit_bytes=48 * 2**20
+            collective_id=0, has_side_effects=True, vmem_limit_bytes=63 * 2**20
         ),
         cost_estimate=pl.CostEstimate(flops=10**9, bytes_accessed=6 * 10**7, transcendentals=10**7),
         name="columns_and_transport",
-    )(block_cost, state, wind_x, wind_y, level_mix, field_mix, jnp.asarray(shifts))
+    )(block_cost.reshape(-1), state, wind_x, wind_y, level_mix, field_mix)
 
 
 def per_device(state, wind_x, wind_y, level_mix, field_mix, block_cost):
     fields, rows, columns, levels = state.shape
     wide_count = lax.axis_size("wide")
     narrow_count = lax.axis_size("narrow")
-    moved, raw, unit, total = whole(
+    moved, raw, total = whole(
         state, wind_x, wind_y, level_mix, field_mix, block_cost, wide_count, narrow_count
     )
-    mean = (total / (rows * columns * wide_count * narrow_count))[:, :, None, :]
-    return (moved - mean * unit[None], raw - mean)
+    count = rows * columns * wide_count * narrow_count
+    return settled(moved, raw, total, count)
+
+
+def settle_kernel(
+    count, step, moved_hbm, raw_hbm, total_ref, state_hbm, tendency_hbm,
+    moved, raw, state, tendency, moved_sem, raw_sem, unit_sem, state_sem, tendency_sem,
+):
+    fields = raw.shape[0]
+    spans = [pl.ds(lo, step) for lo in range(0, fields, step)]
+    moved_loads = [
+        pltpu.make_async_copy(moved_hbm.at[span], moved.at[span], moved_sem.at[index])
+        for index, span in enumerate(spans)
+    ]
+    raw_loads = [
+        pltpu.make_async_copy(raw_hbm.at[span], raw.at[span], raw_sem.at[index])
+        for index, span in enumerate(spans)
+    ]
+    unit_load = pltpu.make_async_copy(moved_hbm.at[fields], moved.at[fields], unit_sem.at[0])
+    unit_load.start()
+    for moved_load, raw_load in zip(moved_loads, raw_loads):
+        raw_load.start()
+        moved_load.start()
+    unit_load.wait()
+    stores = []
+    for index, span in enumerate(spans):
+        raw_loads[index].wait()
+        moved_loads[index].wait()
+        for field in range(index * step, (index + 1) * step):
+            mean = total_ref[field] / np.float32(count)
+            tendency[field] = raw[field] - mean[None]
+            state[field] = moved[field] - mean[None] * moved[fields]
+        for held, target, sem in (
+            (tendency, tendency_hbm, tendency_sem), (state, state_hbm, state_sem),
+        ):
+            stores.append(pltpu.make_async_copy(held.at[span], target.at[span], sem.at[index]))
+            stores[-1].start()
+    for made in stores:
+        made.wait()
+
+
+def settled(moved, raw, total, count):
+    fields, rows, columns, levels = raw.shape
+    step = 2 if fields % 2 == 0 else 1
+    hbm = pl.BlockSpec(memory_space=pltpu.HBM)
+    whole_buffer = pltpu.VMEM(raw.shape, jnp.float32)
+    sems = pltpu.SemaphoreType.DMA((fields // step,))
+    return pl.pallas_call(
+        functools.partial(settle_kernel, count, step),
+        out_shape=(
+            jax.ShapeDtypeStruct(raw.shape, jnp.float32),
+            jax.ShapeDtypeStruct(raw.shape, jnp.float32),
+        ),
+        in_specs=[hbm, hbm, pl.BlockSpec(memory_space=pltpu.VMEM)],
+        out_specs=(hbm, hbm),
+        scratch_shapes=[
+            pltpu.VMEM(moved.shape, jnp.float32), whole_buffer, whole_buffer, whole_buffer,
+            sems, sems, pltpu.SemaphoreType.DMA((1,)), sems, sems,
+        ],
+        compiler_params=pltpu.CompilerParams(vmem_limit_bytes=63 * 2**20),
+        name="settle",
+    )(moved, raw, total)
 
 
 def solution(mesh):

time: 90.1 us -> 56.2 us (0.62)
  Pallas kernels: 81 us -> 55.3 us
  local copies, waits for them, and re-layouts: 6.03 us -> 0 us
  other arithmetic: 1.97 us -> 0 us
    pallas_call x1, Pallas kernels: 81 us -> 51.6 us  [whole(): pl.pallas_call(functools.partial(whole_kernel, wide_count, narrow_count,...]
    unnamed x14 -> x0, local copies, waits for them, and re-layouts: 6.03 us -> none
    pallas_call x0 -> x1, Pallas kernels: none -> 3.69 us  [settled(): pl.pallas_call(functools.partial(settle_kernel, count, step), out_shape=(...]
    sub x1 -> x0, other arithmetic: 1.96 us -> none  [per_device(): return (moved - mean * unit[None], raw - mean)]
where the time goes in v2:
time: 56.2 us; the launch traced here: 55.9 us
  Pallas kernels  55.3 us (98%)
  between operations  0.64 us (1%)
    pallas_call x1, Pallas kernels, whole(): pl.pallas_call(functools.partial(whole_kernel, wide_count, narrow_count,...  51.6 us
    pallas_call x1, Pallas kernels, settled(): pl.pallas_call(functools.partial(settle_kernel, count, step), out_shape=(...  3.69 us

profile of v2, /device:TPU:0, one launch (start us, length us, event | category | flops | bytes accessed | tf_op | source)
XLA Modules:
  0.0 55.9 jit_solution(14586806366768192084)
XLA Ops:
  0.6 51.6 %columns_and_transport.1 = (f32[13,16,16,128]{3,2,1,0:T(8,128)}, f32[12,16,16,128]{3,2,1,0:T(8,128)}, f32[12,1,128]{2,1,0:T(1,128)}) custom-call(s32[2]{0:T(128)} %bitcast.1, f32[12,16,16,128]{3,2,1,0:T(8,128)} %state_hbm.1, bf16[16,16,128]{2,1,0:T(8,128)(2,1)} %wind_x_hbm.1, bf16[16,16,128]{2,1,0:T(8,128)(2,1)} %wind_y_hbm.1, bf16[128,128]{1,0:T(8,128)(2,1)} %level_hbm.1, ...), custom_call_target="tpu_custom_call" | custom-call | flops 1000000000 | bytes 60000000 | tf_op jit(solution)/shard_map/columns_and_transport/pallas_call | solution.py:379
  52.2 3.7 %settle.1 = (f32[12,16,16,128]{3,2,1,0:T(8,128)}, f32[12,16,16,128]{3,2,1,0:T(8,128)}) custom-call(f32[13,16,16,128]{3,2,1,0:T(8,128)} %get-tuple-element.5.moved_hbm, f32[12,16,16,128]{3,2,1,0:T(8,128)} %get-tuple-element.6.raw_hbm, f32[12,1,128]{2,1,0:T(1,128)} %get-tuple-element.7.total_ref), custom_call_target="tpu_custom_call" | custom-call | tf_op jit(solution)/shard_map/settle/pallas_call | solution.py:473
